TPU v7x, 768 devices: a whole 4x8x12 slice. The times are simulated.
768 devices in a mesh: row: 32 (over z_lo, x, core), col: 8 (over y), rep: 3 (over z_hi).
Axes of the slice: x: 4, y: 8, z: 12 (z_hi: 3, z_lo: 4; z = z_hi * 4 + z_lo), core: 2. Of those that a mesh axis runs over, the one named last changes fastest.
Arguments:
- x_tiles: float32 [192, 24, 128, 128], P('row'), may hold values from -6 to 6
- x_mask: int32 [192, 24], P('row'), may hold values 0 or 1
- p_mask: int32 [192, 24], P('row', 'col'), may hold values 0 or 1
- q_mask: int32 [192, 24], P('row', ('col', 'rep')), may hold values 0 or 1
Outputs:
- x_next: float32 [192, 24, 128, 128], P('row', ('col', 'rep'))
All inputs are finite; a program needn't handle non-finite values. No bound on the sum of `x_mask` or of `p_mask` or of `q_mask` on one device may be relied on, other than what follows from the above.
Results may differ from a plain program's by a relative error of at most 0.0033.
Values may be sent and summed in bfloat16 or wider, within the bound.
A program may use at most 128 MiB of HBM per device.

v0:
```python
import math

import jax
import jax.numpy as jnp
import numpy as np
from jax import lax
from jax.sharding import PartitionSpec as P


def from_behind(block, axis, distance):
    devices = range(lax.axis_size(axis))
    route = [((i - distance) % len(devices), i) for i in devices]
    return lax.ppermute(block, axis, route)


def band_lookup(band_tiles, positions):
    band_width = band_tiles.shape[1]
    inside = (positions >= 0) & (positions < band_width)
    clipped = jnp.clip(positions, 0, band_width - 1)
    picked = jax.vmap(lambda tiles_row, where_row: jnp.take(tiles_row, where_row, axis=0))(
        band_tiles, clipped
    )
    return jnp.where(inside[:, :, None, None], picked, jnp.zeros((), band_tiles.dtype))


def tile_einsum(left_tiles, right_tiles):
    return jnp.einsum(
        "imab,miwbc->iwac", left_tiles, right_tiles, preferred_element_type=jnp.float32
    )


def body(x_tiles, x_mask, p_mask, q_mask):
    dev_rows, band_width, tile_order = (x_tiles.shape[0], x_tiles.shape[1], x_tiles.shape[2])
    half_band = band_width // 2
    layers = lax.axis_size("rep")
    columns = lax.axis_size("col")
    col_slice = band_width // columns
    layer_rows = dev_rows // layers
    share_count = col_slice // layers
    reach_span = -(-half_band // dev_rows)
    window_cols = dev_rows + col_slice - 1
    layer_pos = lax.axis_index("rep")
    col_pos = lax.axis_index("col")
    norm_factor = math.sqrt(tile_order * band_width)
    masked = x_tiles * x_mask.astype(jnp.float32)[:, :, None, None]
    scaled = (masked / norm_factor).astype(jnp.bfloat16)
    slot_rows = layer_pos + layers * jnp.arange(layer_rows, dtype=jnp.int32)
    own_rows = jnp.take(scaled, slot_rows, axis=0)
    window_range = jnp.arange(window_cols, dtype=jnp.int32)
    collected = []
    for distance in range(-reach_span, reach_span + 1):
        positions = (
            col_pos * col_slice + window_range[None, :] - dev_rows * distance - slot_rows[:, None]
        )
        sent_piece = band_lookup(own_rows, positions)
        if distance == 0:
            collected.append(sent_piece)
        else:
            collected.append(from_behind(sent_piece, "row", -distance))
    window = jnp.concatenate(collected, axis=0)
    dist_table = np.repeat(np.arange(-reach_span, reach_span + 1), layer_rows).astype(np.int32)
    slot_table = np.tile(np.arange(layer_rows), 2 * reach_span + 1).astype(np.int32)
    row_range = np.arange(dev_rows, dtype=np.int32)
    inner_offset = (
        dev_rows * dist_table[None, :]
        + layers * slot_table[None, :]
        - row_range[:, None]
        + half_band
    ).astype(np.int32) + layer_pos
    pick_cols = row_range[:, None] + np.arange(col_slice, dtype=np.int32)[None, :]
    chosen = window[:, pick_cols]
    first_left = band_lookup(scaled, inner_offset)
    square_part = tile_einsum(first_left, chosen) * p_mask.astype(jnp.float32)[:, :, None, None]
    order_table = (
        (np.arange(layers)[:, None, None] - row_range[None, :, None]) % layers
        + layers * np.arange(share_count)[None, None, :]
    ).astype(np.int32)
    grouped = square_part[row_range[None, :, None], order_table]
    totals = lax.psum(grouped, "rep")
    own_share = lax.dynamic_index_in_dim(totals, layer_pos, 0, keepdims=True)
    square = own_share.astype(jnp.bfloat16)
    gathered = lax.all_gather(square, "col", axis=0, tiled=True)
    flattened = gathered.reshape(columns * dev_rows * share_count, tile_order, tile_order)
    inside = (inner_offset >= 0) & (inner_offset < band_width)
    clipped = jnp.clip(inner_offset, 0, band_width - 1)
    source_col = clipped // col_slice
    within = clipped % col_slice
    linear = (source_col * dev_rows + row_range[:, None]) * share_count + within // layers
    second_left = jnp.take(flattened, linear, axis=0)
    second_left = jnp.where(inside[:, :, None, None], second_left, jnp.zeros((), jnp.bfloat16))
    cube_part = tile_einsum(second_left, chosen)
    cube_sum = lax.psum_scatter(
        cube_part.astype(jnp.bfloat16), "rep", scatter_dimension=1, tiled=True
    ).astype(jnp.float32)
    slice_start = col_pos * col_slice + layer_pos * share_count
    own_masked = lax.dynamic_slice_in_dim(masked, slice_start, share_count, axis=1)
    keep_mask = q_mask.astype(jnp.float32)[:, :, None, None]
    return keep_mask * (1.5 * own_masked - 0.5 * norm_factor * cube_sum)


def solution(mesh):
    in_specs = (
        P("row", None, None, None),
        P("row", None),
        P("row", "col"),
        P("row", ("col", "rep")),
    )
    out_specs = P("row", ("col", "rep"), None, None)
    return jax.shard_map(body, mesh=mesh, in_specs=in_specs, out_specs=out_specs, check_vma=False)
```

profile of v0, /device:TPU:1, one launch (start us, length us, event | category | flops | bytes accessed | tf_op | source)
XLA Modules:
  0.0 331.0 jit_solution(2409454049583471160)
XLA Ops:
  6.6 0.1 bitcast_or_fusion
  6.7 0.6 compare_and_fusion.6
  7.3 0.7 convert_element_type.25
  8.0 0.1 reshape.330
  8.1 9.6 %copy.22 = f32[6,24,128,128]{2,3,1,0:T(8,128)} copy(f32[6,24,128,128]{3,2,1,0:T(8,128)} %param.14) | data formatting | bytes 18874368 | tf_op args[0]
  17.7 10.0 %multiply_convert_fusion = (bf16[6,24,128,128]{2,3,1,0:T(8,128)(2,1)}, f32[6,24,128,128]{2,3,1,0:T(8,128)}) fusion(f32[6,24,128,128]{2,3,1,0:T(8,128)} %copy.22, f32[6,24]{1,0:T(8,128)S(1)} %convert_element_type.25), kind=kLoop, calls=%fused_computation.10 | loop fusion | flops 7077888 | bytes 23593536 | tf_op jit(solution)/shard_map/convert_element_type | solution.py:46
  27.8 3.2 gather_fusion
  31.0 0.2 broadcast_select_fusion
  31.2 0.7 gather_fusion.6
  31.8 1.0 select_select_fusion.3
  32.8 4.5 %collective-permute-start.1 = (bf16[2,8,128,128]{2,3,1,0:T(8,128)(2,1)}, bf16[2,8,128,128]{2,3,1,0:T(8,128)(2,1)}, u32[]{:S(2)}, u32[]{:S(2)}) collective-permute-start(bf16[2,8,128,128]{2,3,1,0:T(8,128)(2,1)} %select_select_fusion.3), channel_id=1, source_target_pairs={{744,0},{0,24},{24,48},{48,72},{72,96},{96,120},{120,144},{144,168... | collective-permute-start | bytes 1572872 | tf_op jit(solution)/shard_map/ppermute | solution.py:13
  37.3 0.1 reshape.325
  37.4 0.7 gather_fusion.5
  38.0 0.9 select_select_fusion.4
  39.0 3.1 collective-permute-start
  42.1 0.1 reshape.340
  42.2 0.7 gather_fusion.8
  42.8 0.9 select_select_fusion.1
  43.8 8.6 %collective-permute-start.2 = (bf16[2,8,128,128]{2,3,1,0:T(8,128)(2,1)}, bf16[2,8,128,128]{2,3,1,0:T(8,128)(2,1)}, u32[]{:S(2)}, u32[]{:S(2)}) collective-permute-start(bf16[2,8,128,128]{2,3,1,0:T(8,128)(2,1)} %select_select_fusion.1), channel_id=1, source_target_pairs={{24,0},{48,24},{72,48},{96,72},{120,96},{144,120},{168,144},{192,1... | collective-permute-start | bytes 1572872 | tf_op jit(solution)/shard_map/ppermute | solution.py:13
  52.4 0.1 reshape.345
  52.5 0.7 gather_fusion.9
  53.1 1.0 select_select_fusion
  54.1 7.5 %collective-permute-start.3 = (bf16[2,8,128,128]{2,3,1,0:T(8,128)(2,1)}, bf16[2,8,128,128]{2,3,1,0:T(8,128)(2,1)}, u32[]{:S(2)}, u32[]{:S(2)}) collective-permute-start(bf16[2,8,128,128]{2,3,1,0:T(8,128)(2,1)} %select_select_fusion), channel_id=1, source_target_pairs={{48,0},{72,24},{96,48},{120,72},{144,96},{168,120},{192,144},{216,... | collective-permute-start | bytes 1572872 | tf_op jit(solution)/shard_map/ppermute | solution.py:13
  61.7 0.6 compare_and_fusion
  62.3 0.7 copy.24
  63.1 0.1 reshape.335
  63.2 3.4 %gather_fusion.4 = bf16[60,128,128]{1,2,0:T(8,128)(2,1)S(1)} fusion(bf16[6,24,128,128]{2,3,1,0:T(8,128)(2,1)} %get-tuple-element.8, s32[60]{0:T(128)S(1)} %reshape.284), kind=kCustom, calls=%fused_computation.9 | custom fusion | bytes 3932640 | tf_op jit(solution)/shard_map/vmap(jit(_take))/gather | solution.py:20
  66.6 2.3 copy.23
  68.8 0.6 gather_fusion.7
  69.5 1.1 constant_dynamic-update-slice_fusion.3
  70.6 1.1 constant_dynamic-update-slice_fusion.2
  71.8 0.4 fusion.34
  72.2 1.1 constant_dynamic-update-slice_fusion.1
  73.3 0.5 collective-permute-done.3
  73.7 1.1 constant_dynamic-update-slice_fusion
  74.9 4.6 %gather_fusion.1 = bf16[18,10,128,128]{2,3,1,0:T(8,128)(2,1)} fusion(bf16[10,8,128,128]{2,3,1,0:T(8,128)(2,1)S(1)} %constant_dynamic-update-slice_fusion, s32[1024]{0:T(1024)S(1)} %pad_clamp_fusion.1), kind=kCustom, calls=%fused_computation.6 | custom fusion | bytes 11796552 | tf_op jit(solution)/shard_map/gather | solution.py:71
  79.5 5.0 %fusion.21 = f32[6,3,128,128]{2,3,1,0:T(8,128)S(1)} fusion(bf16[10,6,3,128,128]{3,4,0,2,1:T(8,128)(2,1)} %bitcast.94, bf16[6,10,128,128]{3,2,1,0:T(8,128)(2,1)} %copy.23, pred[6,10]{1,0:T(8,128)(4,1)S(1)} %copy-done.8, pred[6,10]{1,0:T(8,128)(4,1)S(1)} %copy-done.7, f32[6,3]{1,0:T(8,128)S(1)} %copy-done.2), kind=kOutput, calls=%fused_computation.28 | convolution fusion | flops 757235712 | bytes 9044160 | tf_op jit(solution)/shard_map/imab,miwbc->iwac/dot_general | solution.py:27
  84.5 0.7 gather_fusion.2
  85.2 0.4 copy.25
  85.6 93.3 %all-reduce.5 = bf16[3,6,1,128,128]{4,3,2,1,0:T(8,128)(2,1)S(1)} all-reduce(f32[3,6,1,128,128]{4,3,2,1,0:T(8,128)S(1)} %copy.25), channel_id=1, replica_groups=mesh['row'=32,'col'=8,'rep'=3] {'rep'}, use_global_device_ids=true, to_apply=%region_0.0 | all-reduce | flops 294912 | bytes 1769472 | tf_op jit(solution)/shard_map/psum | solution.py:79
  178.9 0.7 dynamic-slice_convert_fusion
  179.7 54.6 %all-gather.2.cloned.1.call-done = bf16[8,6,1,128,128]{4,3,2,1,0:T(8,128)(2,1)} async-done(((bf16[1,6,1,128,128]{4,3,2,1,0:T(8,128)(2,1)}), bf16[8,6,1,128,128]{4,3,2,1,0:T(8,128)(2,1)}) %all-gather.2.cloned.1.call-update) | async-done | bytes 1572880 | tf_op jit(solution)/shard_map/all_gather | solution.py:82
  234.3 2.3 gather_fusion.3
  236.7 5.3 %fusion.27 = bf16[6,3,128,128]{2,3,1,0:T(8,128)(2,1)} fusion(bf16[10,6,3,128,128]{3,4,0,2,1:T(8,128)(2,1)} %bitcast.95, bf16[6,10,128,128]{3,2,1,0:T(8,128)(2,1)S(1)} %bitcast.103, pred[6,10]{1,0:T(8,128)(4,1)S(1)} %copy-done.6, pred[6,10]{1,0:T(8,128)(4,1)S(1)} %copy-done.7), kind=kOutput, calls=%fused_computation.30 | convolution fusion | flops 757235712 | bytes 8454264 | tf_op jit(solution)/shard_map/imab,miwbc->iwac/dot_general | solution.py:27
  242.0 1.3 dynamic-slice
  243.3 78.2 %all-reduce.4.cloned.1.call-done = bf16[6,3,128,128]{2,3,1,0:T(8,128)(2,1)} async-done(((bf16[6,3,128,128]{2,3,1,0:T(8,128)(2,1)}), bf16[6,3,128,128]{2,3,1,0:T(8,128)(2,1)}) %all-reduce.4.cloned.1.call-update) | async-done | bytes 589840
  321.5 1.8 subtract_multiply_fusion
  323.3 0.9 copy.26
  (43 shorter events, 0.4 us)
Async XLA Ops:
  6.5 227.8 %all-gather.2.cloned.1.call-start = ((), (), s32[]{:S(2)}) async-start(), calls=%async_computation | async-start | bytes 1769472 | tf_op jit(solution)/shard_map/all_gather | solution.py:82
  32.8 37.8 %collective-permute-start.1 = (bf16[2,8,128,128]{2,3,1,0:T(8,128)(2,1)}, bf16[2,8,128,128]{2,3,1,0:T(8,128)(2,1)}, u32[]{:S(2)}, u32[]{:S(2)}) collective-permute-start(bf16[2,8,128,128]{2,3,1,0:T(8,128)(2,1)} %select_select_fusion.3), channel_id=1, source_target_pairs={{744,0},{0,24},{24,48},{48,72},{72,96},{96,120},{120,144},{144,168... | collective-permute-start | bytes 1572872 | tf_op jit(solution)/shard_map/ppermute | solution.py:13
  39.0 30.5 %collective-permute-start = (bf16[2,8,128,128]{2,3,1,0:T(8,128)(2,1)}, bf16[2,8,128,128]{2,3,1,0:T(8,128)(2,1)}, u32[]{:S(2)}, u32[]{:S(2)}) collective-permute-start(bf16[2,8,128,128]{2,3,1,0:T(8,128)(2,1)} %select_select_fusion.4), channel_id=1, source_target_pairs={{720,0},{744,24},{0,48},{24,72},{48,96},{72,120},{96,144},{120,168... | collective-permute-start | bytes 1572872 | tf_op jit(solution)/shard_map/ppermute | solution.py:13
  42.2 19.5 %copy-start.1 = (s32[6,10]{1,0:T(8,128)S(1)}, s32[6,10]{1,0:T(8,128)}, u32[]{:S(2)}) copy-start(s32[6,10]{1,0:T(8,128)} %constant.135.clone) | copy-start | bytes 724
  42.2 20.1 %copy-start.9 = (s32[18]{0:T(128)S(1)}, s32[18]{0:T(128)}, u32[]{:S(2)}) copy-start(s32[18]{0:T(128)} %constant.241) | copy-start | bytes 220
  42.2 20.1 %copy-start.5 = (s32[6,3]{0,1:T(4,128)S(1)}, s32[6,3]{0,1:T(4,128)}, u32[]{:S(2)}) copy-start(s32[6,3]{0,1:T(4,128)} %param.16) | copy-start | bytes 220
  43.8 28.4 %collective-permute-start.2 = (bf16[2,8,128,128]{2,3,1,0:T(8,128)(2,1)}, bf16[2,8,128,128]{2,3,1,0:T(8,128)(2,1)}, u32[]{:S(2)}, u32[]{:S(2)}) collective-permute-start(bf16[2,8,128,128]{2,3,1,0:T(8,128)(2,1)} %select_select_fusion.1), channel_id=1, source_target_pairs={{24,0},{48,24},{72,48},{96,72},{120,96},{144,120},{168,144},{192,1... | collective-permute-start | bytes 1572872 | tf_op jit(solution)/shard_map/ppermute | solution.py:13
  54.1 19.6 %collective-permute-start.3 = (bf16[2,8,128,128]{2,3,1,0:T(8,128)(2,1)}, bf16[2,8,128,128]{2,3,1,0:T(8,128)(2,1)}, u32[]{:S(2)}, u32[]{:S(2)}) collective-permute-start(bf16[2,8,128,128]{2,3,1,0:T(8,128)(2,1)} %select_select_fusion), channel_id=1, source_target_pairs={{48,0},{72,24},{96,48},{120,72},{144,96},{168,120},{192,144},{216,... | collective-permute-start | bytes 1572872 | tf_op jit(solution)/shard_map/ppermute | solution.py:13
  68.8 2.9 copy-start.3
  68.8 2.9 copy-start.4
  74.9 4.6 %copy-start.2 = (f32[6,3]{1,0:T(8,128)S(1)}, f32[6,3]{1,0:T(8,128)}, u32[]{:S(2)}) copy-start(f32[6,3]{1,0:T(8,128)} %copy.24) | copy-start | bytes 220
  74.9 4.6 %copy-start.7 = (pred[6,10]{1,0:T(8,128)(4,1)S(1)}, pred[6,10]{1,0:T(8,128)(4,1)}, u32[]{:S(2)}) copy-start(pred[6,10]{1,0:T(8,128)(4,1)} %get-tuple-element.11) | copy-start | bytes 184
  74.9 4.6 %copy-start.8 = (pred[6,10]{1,0:T(8,128)(4,1)S(1)}, pred[6,10]{1,0:T(8,128)(4,1)}, u32[]{:S(2)}) copy-start(pred[6,10]{1,0:T(8,128)(4,1)} %get-tuple-element.10) | copy-start | bytes 184
  79.5 5.1 %copy-start = (s32[18]{0:T(128)S(1)}, s32[18]{0:T(128)}, u32[]{:S(2)}) copy-start(s32[18]{0:T(128)} %constant.250) | copy-start | bytes 220
  179.6 141.9 %all-reduce.4.cloned.1.call-start = ((), (), s32[]{:S(2)}) async-start(), calls=%async_computation.1 | async-start | bytes 1179648
  234.3 2.3 copy-start.6
  236.7 6.6 %copy-start.10 = (s32[6,1]{0,1:T(1,128)S(1)}, s32[6,1]{0,1:T(1,128)}, u32[]{:S(2)}) copy-start(s32[6,1]{0,1:T(1,128)} %param.17) | copy-start | bytes 76
Sparse Core Ops, SparseCore 0:
  179.7 54.5 all-gather.1
  242.1 79.3 all-reduce.3
where the time goes:
time: 334 us; the launch traced here: 331 us
  waiting for transfers between devices  133 us (40%)
  blocking collectives  93.3 us (28%)
  local copies, waits for them, and re-layouts  38.3 us (11%)
  starting transfers between devices  23.8 us (7%)
  other arithmetic  18.3 us (5%)
  between operations  13.8 us (4%)
  matrix products  10.3 us (3%)
    psum x1, blocking collectives, body(): totals = lax.psum(grouped, 'rep')  93.3 us
    unnamed x3, waiting for transfers between devices  78.3 us
    all_gather x1, waiting for transfers between devices, body(): gathered = lax.all_gather(square, 'col', axis=0, tiled=True)  54.6 us
    ppermute x4, starting transfers between devices, from_behind(): return lax.ppermute(block, axis, route)  23.8 us
    unnamed x27, local copies, waits for them, and re-layouts  14.3 us
    dot_general x2, matrix products, tile_einsum(): jnp.einsum('imab,miwbc->iwac', left_tiles, right_tiles, preferred_element...  10.3 us
    convert_element_type x1, other arithmetic, body(): scaled = (masked / norm_factor).astype(jnp.bfloat16)  10 us
    gather x13, local copies, waits for them, and re-layouts, band_lookup(): jnp.take(tiles_row, where_row, axis=0)  9.41 us
  transfers between devices with their start and end apart: 6, of which 3 were waited for; matrix products, arithmetic and copies ran while one was open for 5% of the time, Pallas kernels for 0%

commit v1 on v0

v1 whole, which is shorter than its diff:
```python
import math

import jax
import jax.numpy as jnp
from jax import lax
from jax.experimental import pallas as pl
from jax.experimental.pallas import tpu as pltpu
from jax.sharding import PartitionSpec as P

MESH = pl.DeviceIdType.MESH
F32, BF16 = jnp.float32, jnp.bfloat16


def kernel(T, BW, n_rows, xm, pm, qm, x_hbm, out, xf, S, R, L, Q, PM, C, fin,
           ld_sem, x_send, x_recv, sib_send, sib_recv, pm_send, pm_recv,
           r_send, r_recv, f_send, f_recv):
    row, c, p = lax.axis_index("row"), lax.axis_index("col"), lax.axis_index("rep")
    n_chip = n_rows // 2
    q, s = lax.div(row, 2), lax.rem(row, 2)
    norm = math.sqrt(T * BW)
    inv_norm = 1.0 / norm
    p_fwd = jnp.where(q == n_chip - 1, lax.rem(p + 1, 3), p)
    p_bwd = jnp.where(q == 0, lax.rem(p + 2, 3), p)
    fwd = (lax.rem(row + 2, n_rows), c, p_fwd)
    bwd = (lax.rem(row + n_rows - 2, n_rows), c, p_bwd)
    sib = (row + 1 - 2 * s, c, p)
    right = (row, lax.rem(c + 1, 8), p)
    left = (row, lax.rem(c + 7, 8), p)
    w_me = 3 * c + p

    for k in range(6):
        pltpu.make_async_copy(x_hbm.at[k], xf.at[k], ld_sem.at[k]).start()

    def band_of(src, a, e):
        return lax.rem(lax.rem(src + 2 * s, 8) + 8 - a, 8) + 8 * e

    barrier = pltpu.get_barrier_semaphore()
    for peer in (fwd, bwd, sib):
        pl.semaphore_signal(barrier, inc=1, device_id=peer, device_id_type=MESH)
    for d in range(1, 8):
        pl.semaphore_signal(barrier, inc=1, device_id=(row, lax.rem(c + d, 8), p), device_id_type=MESH)

    def source_of(i):
        return lax.rem(w_me + i % 2 + 8 - 2 * s, 8)

    for i in range(6):
        src = source_of(i)

        @pl.when(jnp.logical_not((src == c) & (i // 2 == p)))
        def _():
            pl.semaphore_signal(barrier, inc=1, device_id=(row, src, jnp.int32(i // 2)), device_id_type=MESH)

    targets = []
    n_out = jnp.int32(0)
    for a in range(2):
        for e in range(3):
            w = band_of(c, a, e)
            cd, pd = lax.div(w, 3), lax.rem(w, 3)
            own = (cd == c) & (pd == p)
            targets.append((cd, pd, own))
            n_out = n_out + jnp.where(own, 0, 1)

    PM[c] = jnp.zeros((8, T), F32)
    for wl in range(3):
        for a in range(2):
            PM[c, pl.ds(wl * 2 + a, 1), :] = jnp.full((1, T), pm[2 * p + a, wl].astype(F32), F32)
    R[3, pl.ds(0, 12 * T), :] = jnp.zeros((12 * T, T), BF16)
    R[0, pl.ds(24 * T, 12 * T), :] = jnp.zeros((12 * T, T), BF16)

    def tile(k, w):
        ok = (w >= 0) & (w < BW)
        wc = jnp.clip(w, 0, BW - 1)
        scale = jnp.where(ok, xm[k, wc].astype(F32) * inv_norm, 0.0)
        return (xf[k, wc] * scale).astype(BF16)

    for k in range(6):
        pltpu.make_async_copy(x_hbm.at[k], xf.at[k], ld_sem.at[k]).wait()

        @pl.loop(0, 6)
        def _(h):
            base = jnp.where(h < 3, 2 * p_fwd + 12 + 8 * h, 2 * p_bwd - 12 + 8 * (h - 2)) + c - 6 * s
            S[h, pl.ds(k * T, T), :] = tile(k, base - k)

    pl.semaphore_wait(barrier, 10 + n_out)

    def x_copy(h):
        m = h if h < 3 else h - 2
        place = (0 if h < 3 else 24) + 6 * s
        return pltpu.make_async_remote_copy(
            src_ref=S.at[h], dst_ref=R.at[m, pl.ds(pl.multiple_of(place * T, T), 6 * T)],
            send_sem=x_send.at[h], recv_sem=x_recv.at[h],
            device_id=fwd if h < 3 else bwd, device_id_type=MESH)

    for h in (0, 3, 1, 4, 2, 5):
        x_copy(h).start()

    def pm_copy(d):
        return pltpu.make_async_remote_copy(
            src_ref=PM.at[c], dst_ref=PM.at[c], send_sem=pm_send.at[d - 1], recv_sem=pm_recv.at[d - 1],
            device_id=(row, lax.rem(c + d, 8), p), device_id_type=MESH)

    for d in range(1, 8):
        pm_copy(d).start()

    @pl.loop(0, 4)
    def _(m):
        for k in range(6):
            at = pl.multiple_of((12 + 6 * s + k) * T, T)
            R[m, pl.ds(at, T), :] = tile(k, 2 * p + c - 6 * s + 8 * m - k)

    def sib_copy(i, half):
        if i < 4:
            m, place = i, 12
        else:
            h = i - 4
            m, place = (h, 0) if h < 3 else (h - 2, 24)
        part = R.at[m, pl.ds(pl.multiple_of((place + 6 * half) * T, T), 6 * T)]
        return pltpu.make_async_remote_copy(
            src_ref=part, dst_ref=part, send_sem=sib_send.at[i], recv_sem=sib_recv.at[i],
            device_id=sib, device_id_type=MESH)

    for m in range(4):
        sib_copy(m, s).start()

    @pl.loop(0, BW)
    def _(u):
        for a in range(2):
            L[a, :, pl.ds(pl.multiple_of(u * T, T), T)] = tile(2 * p + a, u)

    for d in range(1, 8):
        pm_copy(d).wait_recv()

    w0 = [band_of(c, a, 0) for a in range(2)]
    m0 = [lax.div(w0[a] + a + 6 * s - c, 8) for a in range(2)]

    def column(a, e):
        start = pl.multiple_of((6 * s + 2 * p + a) * T, T)
        return R[m0[a] + e, pl.ds(start, BW * T), :]

    def ring_copy(way, h, a, e, src):
        w = band_of(src, a, e)
        part = Q.at[a, :, pl.ds(pl.multiple_of(w * T, T), T)]
        j = a * 3 + e
        return pltpu.make_async_remote_copy(
            src_ref=part, dst_ref=part, send_sem=r_send.at[way, h - 1, j], recv_sem=r_recv.at[way, h - 1, j],
            device_id=right if way == 0 else left, device_id_type=MESH)

    def source(way, h):
        return lax.rem(c + 8 - (h - 1), 8) if way == 0 else lax.rem(c + h - 1, 8)

    def halves(way, h):
        return (0, 1) if h < 4 else (way,)

    def arrive(m):
        hs = ([m] if m < 3 else []) + ([m + 2] if m > 0 else [])
        for h in hs:
            x_copy(h).wait_recv()
            sib_copy(4 + h, s).start()
        return hs

    for e in range(3):
        ms = (0, 1) if e == 0 else (e + 1,)
        hss = [arrive(m) for m in ms]
        for m, hs in zip(ms, hss):
            sib_copy(m, 1 - s).wait_recv()
            for h in hs:
                sib_copy(4 + h, 1 - s).wait_recv()
        for a in range(2):
            acc = jnp.dot(L[a], column(a, e), preferred_element_type=F32)
            w = w0[a] + 8 * e
            keep = PM[lax.div(w, 3), pl.ds(lax.rem(w, 3) * 2 + a, 1), :]
            Q[a, :, pl.ds(pl.multiple_of(w * T, T), T)] = (acc * keep).astype(BF16)
            for way in range(2):
                ring_copy(way, 1, a, e, source(way, 1)).start()

    for h in range(1, 5):
        for e in range(3):
            for way in range(2):
                for a in halves(way, h):
                    ring_copy(way, h, a, e, source(way, h + 1)).wait_recv()
                    if h < 4 and a in halves(way, h + 1):
                        ring_copy(way, h + 1, a, e, source(way, h + 1)).start()

    for a in range(2):
        for e in range(3):
            j = a * 3 + e
            cd, pd, own = targets[j]
            value = jnp.dot(Q[a], column(a, e), preferred_element_type=F32).astype(BF16)
            C[j] = value

            @pl.when(own)
            def _():
                fin[2 * p + a] = value

            @pl.when(jnp.logical_not(own))
            def _():
                pltpu.make_async_remote_copy(
                    src_ref=C.at[j], dst_ref=fin.at[2 * p + a], send_sem=f_send.at[j],
                    recv_sem=f_recv.at[2 * p + a], device_id=(row, cd, pd), device_id_type=MESH).start()

    for i in range(6):
        @pl.when(jnp.logical_not((source_of(i) == c) & (i // 2 == p)))
        def _():
            pltpu.make_async_remote_copy(
                src_ref=C.at[0], dst_ref=fin.at[i], send_sem=f_send.at[0], recv_sem=f_recv.at[i],
                device_id=right, device_id_type=MESH).wait_recv()

        keep = qm[i, 0].astype(F32)
        masked = xf[i, w_me] * xm[i, w_me].astype(F32)
        out[i, 0] = keep * (1.5 * masked - (0.5 * norm) * fin[i].astype(F32))

    for h in range(6):
        x_copy(h).wait_send()
    for d in range(1, 8):
        pm_copy(d).wait_send()
    for i in range(10):
        sib_copy(i, s).wait_send()
    for h in range(1, 5):
        for e in range(3):
            for way in range(2):
                for a in halves(way, h):
                    ring_copy(way, h, a, e, source(way, h)).wait_send()
    for j in range(6):
        @pl.when(jnp.logical_not(targets[j][2]))
        def _():
            pltpu.make_async_remote_copy(
                src_ref=C.at[j], dst_ref=fin.at[0], send_sem=f_send.at[j], recv_sem=f_recv.at[0],
                device_id=right, device_id_type=MESH).wait_send()


def body(x_tiles, x_mask, p_mask, q_mask):
    rows, BW, T = x_tiles.shape[0], x_tiles.shape[1], x_tiles.shape[2]
    n_rows = lax.axis_size("row")
    dma = pltpu.SemaphoreType.DMA

    def run(*refs):
        kernel(T, BW, n_rows, *refs)

    return pl.pallas_call(
        run,
        out_shape=jax.ShapeDtypeStruct((rows, 1, T, T), F32),
        in_specs=[pl.BlockSpec(memory_space=pltpu.SMEM)] * 3 + [pl.BlockSpec(memory_space=pl.ANY)],
        out_specs=pl.BlockSpec(memory_space=pltpu.VMEM),
        scratch_shapes=[
            pltpu.VMEM((rows, BW, T, T), F32),
            pltpu.VMEM((6, 6 * T, T), BF16),
            pltpu.VMEM((4, 36 * T, T), BF16),
            pltpu.VMEM((2, T, BW * T), BF16),
            pltpu.VMEM((2, T, BW * T), BF16),
            pltpu.VMEM((8, 8, T), F32),
            pltpu.VMEM((6, T, T), BF16),
            pltpu.VMEM((6, T, T), BF16),
            dma((6,)), dma((6,)), dma((6,)), dma((10,)), dma((10,)), dma((7,)), dma((7,)),
            dma((2, 4, 6)), dma((2, 4, 6)), dma((6,)), dma((6,)),
        ],
        compiler_params=pltpu.CompilerParams(
            collective_id=0, has_side_effects=True, vmem_limit_bytes=56 * 1024 * 1024),
        name="sign_step",
    )(x_mask, p_mask, q_mask, x_tiles)


def solution(mesh):
    in_specs = (
        P("row", None, None, None),
        P("row", None),
        P("row", "col"),
        P("row", ("col", "rep")),
    )
    out_specs = P("row", ("col", "rep"), None, None)
    return jax.shard_map(body, mesh=mesh, in_specs=in_specs, out_specs=out_specs, check_vma=False)
```

time: 334 us -> 72.9 us (0.22)
  waiting for transfers between devices: 133 us -> 0 us
  blocking collectives: 93.3 us -> 0 us
  Pallas kernels: 0 us -> 68.3 us
  local copies, waits for them, and re-layouts: 38.3 us -> 4.44 us
  starting transfers between devices: 23.8 us -> 0 us
  other arithmetic: 18.3 us -> 0 us
  between operations: 13.8 us -> 0.01 us
  matrix products: 10.3 us -> 0 us
    psum x1 -> x0, blocking collectives: 93.3 us -> none  [body(): totals = lax.psum(grouped, 'rep')]
    unnamed x3 -> x0, waiting for transfers between devices: 78.3 us -> none
    pallas_call x0 -> x1, Pallas kernels: none -> 68.3 us  [body(): pl.pallas_call(run, out_shape=jax.ShapeDtypeStruct((rows, 1, T, T), F32),...]
    all_gather x1 -> x0, waiting for transfers between devices: 54.6 us -> none  [body(): gathered = lax.all_gather(square, 'col', axis=0, tiled=True)]
    ppermute x4 -> x0, starting transfers between devices: 23.8 us -> none  [from_behind(): return lax.ppermute(block, axis, route)]
    gather x18 -> x0, local copies, waits for them, and re-layouts: 20.5 us -> none  [the longest x13 9.41 us: band_lookup(): jnp.take(tiles_row, where_row, axis=0)]
    convert_element_type x3 -> x0, other arithmetic: 10.7 us -> none  [the longest x1 10 us: body(): scaled = (masked / norm_factor).astype(jnp.bfloat16)]
    dot_general x2 -> x0, matrix products: 10.3 us -> none  [tile_einsum(): jnp.einsum('imab,miwbc->iwac', left_tiles, right_tiles, preferred_element...]
  transfers between devices with their start and end apart: 6 -> 0, of which waited for: 3 -> 0; matrix products, arithmetic and copies ran while one was open for 5% -> 0% of each run, Pallas kernels for 0% -> 0%
where the time goes in v1:
time: 72.9 us; the launch traced here: 72.7 us
  Pallas kernels  68.3 us (94%)
  local copies, waits for them, and re-layouts  4.44 us (6%)
    pallas_call x1, Pallas kernels, body(): pl.pallas_call(run, out_shape=jax.ShapeDtypeStruct((rows, 1, T, T), F32),...  68.3 us
    unnamed x3, local copies, waits for them, and re-layouts  4.44 us

profile of v1, /device:TPU:1, one launch (start us, length us, event | category | flops | bytes accessed | tf_op | source)
XLA Modules:
  0.0 72.7 jit_solution(946467206645426064)
XLA Ops:
  0.0 1.4 %copy.5.refs_1_ = s32[6,3]{1,0:T(8,128)} copy(s32[6,3]{0,1:T(4,128)} %param.6) | data formatting | bytes 144 | tf_op args[2]
  1.4 1.3 %copy.6.refs_2_ = s32[6,1]{1,0:T(8,128)} copy(s32[6,1]{0,1:T(1,128)} %param.7) | data formatting | bytes 48 | tf_op args[3]
  2.7 68.3 %sign_step.1 = f32[6,1,128,128]{3,2,1,0:T(8,128)} custom-call(s32[6,24]{1,0:T(8,128)} %refs_0_.1, s32[6,3]{1,0:T(8,128)} %copy.5.refs_1_, s32[6,1]{1,0:T(8,128)} %copy.6.refs_2_, f32[6,24,128,128]{3,2,1,0:T(8,128)} %refs_3_.1), custom_call_target="tpu_custom_call" | custom-call | tf_op jit(solution)/shard_map/sign_step/pallas_call | solution.py:239
  70.9 1.8 %copy.8 = f32[6,1,128,128]{3,2,1,0:T(8,128)} copy(f32[6,1,128,128]{3,2,1,0:T(8,128)} %sign_step.1) | data formatting | bytes 786432

commit v2 on v1

v2 whole, which is shorter than its diff:
```python
import math

import jax
import jax.numpy as jnp
from jax import lax
from jax.experimental import pallas as pl
from jax.experimental.pallas import tpu as pltpu
from jax.sharding import PartitionSpec as P

MESH = pl.DeviceIdType.MESH
F32, BF16 = jnp.float32, jnp.bfloat16


def kernel(T, BW, n_rows, xm, pm, qm, x_hbm, out, xs, xo, xl, xf, S, R, L, Q, PM, C, fin,
           ls_sem, lo_sem, ll_sem, lf_sem, x_send, x_recv, sib_send, sib_recv, pm_send, pm_recv,
           r_send, r_recv, f_send, f_recv):
    row, c, p = lax.axis_index("row"), lax.axis_index("col"), lax.axis_index("rep")
    n_chip = n_rows // 2
    q, s = lax.div(row, 2), lax.rem(row, 2)
    norm = math.sqrt(T * BW)
    inv_norm = 1.0 / norm
    p_fwd = jnp.where(q == n_chip - 1, lax.rem(p + 1, 3), p)
    p_bwd = jnp.where(q == 0, lax.rem(p + 2, 3), p)
    fwd = (lax.rem(row + 2, n_rows), c, p_fwd)
    bwd = (lax.rem(row + n_rows - 2, n_rows), c, p_bwd)
    sib = (row + 1 - 2 * s, c, p)
    right = (row, lax.rem(c + 1, 8), p)
    left = (row, lax.rem(c + 7, 8), p)
    w_me = 3 * c + p

    def halo_base(h):
        return (2 * p_fwd + 12 + 8 * h if h < 3 else 2 * p_bwd - 12 + 8 * (h - 2)) + c - 6 * s

    def own_base(m):
        return 2 * p + c - 6 * s + 8 * m

    def load(base, buf, sem):
        @pl.loop(0, 6)
        def _(k):
            pltpu.make_async_copy(x_hbm.at[k, jnp.clip(base - k, 0, BW - 1)], buf.at[k], sem).start()

    def loaded(buf, sem):
        pltpu.make_async_copy(x_hbm.at[pl.ds(0, 6), 0], buf, sem).wait()

    for h in (1, 3):
        load(halo_base(h), xs.at[h], ls_sem.at[h])
    load(own_base(1), xo.at[1], lo_sem.at[1])
    for h in (2, 4):
        load(halo_base(h), xs.at[h], ls_sem.at[h])
    rows_copy = pltpu.make_async_copy(x_hbm.at[pl.ds(2 * p, 2)], xl, ll_sem)
    rows_copy.start()
    load(own_base(2), xo.at[2], lo_sem.at[2])
    for h in (0, 5):
        load(halo_base(h), xs.at[h], ls_sem.at[h])
    for m in (0, 3):
        load(own_base(m), xo.at[m], lo_sem.at[m])
    final_copy = pltpu.make_async_copy(x_hbm.at[pl.ds(0, 6), w_me], xf, lf_sem)
    final_copy.start()

    def first_of(src, a):
        return lax.rem(lax.rem(src + 2 * s, 8) + 8 - a, 8)

    barrier = pltpu.get_barrier_semaphore()
    for peer in (fwd, bwd, sib):
        pl.semaphore_signal(barrier, inc=1, device_id=peer, device_id_type=MESH)
    for d in range(1, 8):
        pl.semaphore_signal(barrier, inc=1, device_id=(row, lax.rem(c + d, 8), p), device_id_type=MESH)

    def source_of(i):
        return lax.rem(w_me + i % 2 + 8 - 2 * s, 8)

    for i in range(6):
        src = source_of(i)

        @pl.when(jnp.logical_not((src == c) & (i // 2 == p)))
        def _():
            pl.semaphore_signal(barrier, inc=1, device_id=(row, src, jnp.int32(i // 2)), device_id_type=MESH)

    targets = []
    n_out = jnp.int32(0)
    for a in range(2):
        for e in range(3):
            w = first_of(c, a) + 8 * e
            cd, pd = lax.div(w, 3), lax.rem(w, 3)
            own = (cd == c) & (pd == p)
            targets.append((cd, pd, own))
            n_out = n_out + jnp.where(own, 0, 1)

    def scale_of(k, w):
        ok = (w >= 0) & (w < BW)
        return jnp.where(ok, xm[k, jnp.clip(w, 0, BW - 1)].astype(F32) * inv_norm, 0.0)

    def make_halo(h):
        base = halo_base(h)
        loaded(xs.at[h], ls_sem.at[h])

        @pl.loop(0, 6)
        def _(k):
            S[h, pl.ds(pl.multiple_of(k * T, T), T), :] = (xs[h, k] * scale_of(k, base - k)).astype(BF16)

    def make_own(m):
        base = own_base(m)
        loaded(xo.at[m], lo_sem.at[m])

        @pl.loop(0, 6)
        def _(k):
            at = pl.multiple_of((12 + 6 * s + k) * T, T)
            R[m, pl.ds(at, T), :] = (xo[m, k] * scale_of(k, base - k)).astype(BF16)

    def x_copy(h):
        m = h if h < 3 else h - 2
        place = (0 if h < 3 else 24) + 6 * s
        return pltpu.make_async_remote_copy(
            src_ref=S.at[h], dst_ref=R.at[m, pl.ds(pl.multiple_of(place * T, T), 6 * T)],
            send_sem=x_send.at[h], recv_sem=x_recv.at[h],
            device_id=fwd if h < 3 else bwd, device_id_type=MESH)

    def pm_copy(d):
        return pltpu.make_async_remote_copy(
            src_ref=PM.at[c], dst_ref=PM.at[c], send_sem=pm_send.at[d - 1], recv_sem=pm_recv.at[d - 1],
            device_id=(row, lax.rem(c + d, 8), p), device_id_type=MESH)

    def sib_copy(i, half):
        if i < 4:
            m, place = i, 12
        else:
            h = i - 4
            m, place = (h, 0) if h < 3 else (h - 2, 24)
        part = R.at[m, pl.ds(pl.multiple_of((place + 6 * half) * T, T), 6 * T)]
        return pltpu.make_async_remote_copy(
            src_ref=part, dst_ref=part, send_sem=sib_send.at[i], recv_sem=sib_recv.at[i],
            device_id=sib, device_id_type=MESH)

    make_halo(1)
    make_halo(3)
    pl.semaphore_wait(barrier, 10 + n_out)
    x_copy(1).start()
    x_copy(3).start()
    PM[c] = jnp.zeros((8, T), F32)
    for wl in range(3):
        for a in range(2):
            PM[c, pl.ds(wl * 2 + a, 1), :] = jnp.full((1, T), pm[wl, 2 * p + a].astype(F32), F32)
    for d in range(1, 8):
        pm_copy(d).start()
    for h in (2, 4):
        make_halo(h)
        x_copy(h).start()
    make_own(1)
    sib_copy(1, s).start()
    for h in (0, 5):
        make_halo(h)
        x_copy(h).start()
    rows_copy.wait()

    @pl.loop(0, BW)
    def _(u):
        for a in range(2):
            L[a, :, pl.ds(pl.multiple_of(u * T, T), T)] = (xl[a, u] * scale_of(2 * p + a, u)).astype(BF16)

    for m in (2, 0, 3):
        make_own(m)
        sib_copy(m, s).start()
    R[3, pl.ds(0, 12 * T), :] = jnp.zeros((12 * T, T), BF16)
    R[0, pl.ds(24 * T, 12 * T), :] = jnp.zeros((12 * T, T), BF16)

    for d in range(1, 8):
        pm_copy(d).wait_recv()

    def place_of(src, a, o):
        w0 = first_of(src, a)
        m0 = lax.div(w0 + a + 6 * s - src, 8)
        e = (1 - m0, 2 - m0, 2 * m0)[o]
        return w0 + 8 * e, m0 + e

    def column(a, m):
        start = pl.multiple_of((6 * s + 2 * p + a) * T, T)
        return R[m, pl.ds(start, BW * T), :]

    def ring_copy(way, h, a, o, src):
        w, _ = place_of(src, a, o)
        part = Q.at[a, :, pl.ds(pl.multiple_of(w * T, T), T)]
        j = a * 3 + o
        return pltpu.make_async_remote_copy(
            src_ref=part, dst_ref=part, send_sem=r_send.at[way, h - 1, j], recv_sem=r_recv.at[way, h - 1, j],
            device_id=right if way == 0 else left, device_id_type=MESH)

    def source(way, h):
        return lax.rem(c + 8 - (h - 1), 8) if way == 0 else lax.rem(c + h - 1, 8)

    def halves(way, h):
        return (0, 1) if h < 4 else (way,)

    def square_round(o):
        hs, ms = (((1, 3), (1,)), ((2, 4), (2,)), ((0, 5), (0, 3)))[o]
        for h in hs:
            x_copy(h).wait_recv()
            sib_copy(4 + h, s).start()
        for m in ms:
            sib_copy(m, 1 - s).wait_recv()
        for h in hs:
            sib_copy(4 + h, 1 - s).wait_recv()
        for a in range(2):
            w, m = place_of(c, a, o)
            acc = jnp.dot(L[a], column(a, m), preferred_element_type=F32)
            keep = PM[lax.div(w, 3), pl.ds(lax.rem(w, 3) * 2 + a, 1), :]
            Q[a, :, pl.ds(pl.multiple_of(w * T, T), T)] = (acc * keep).astype(BF16)
            for way in range(2):
                ring_copy(way, 1, a, o, source(way, 1)).start()

    def ring_step(h, o):
        for way in range(2):
            for a in halves(way, h):
                ring_copy(way, h, a, o, source(way, h + 1)).wait_recv()
                if h < 4 and a in halves(way, h + 1):
                    ring_copy(way, h + 1, a, o, source(way, h + 1)).start()

    square_round(0)
    ring_step(1, 0)
    square_round(1)
    ring_step(2, 0)
    ring_step(1, 1)
    square_round(2)
    for h, o in ((3, 0), (2, 1), (1, 2), (4, 0), (3, 1), (2, 2), (4, 1), (3, 2), (4, 2)):
        ring_step(h, o)

    for a in range(2):
        for e in range(3):
            j = a * 3 + e
            cd, pd, own = targets[j]
            w0 = first_of(c, a)
            m = lax.div(w0 + a + 6 * s - c, 8) + e
            value = jnp.dot(Q[a], column(a, m), preferred_element_type=F32).astype(BF16)
            C[j] = value

            @pl.when(own)
            def _():
                fin[2 * p + a] = value

            @pl.when(jnp.logical_not(own))
            def _():
                pltpu.make_async_remote_copy(
                    src_ref=C.at[j], dst_ref=fin.at[2 * p + a], send_sem=f_send.at[j],
                    recv_sem=f_recv.at[2 * p + a], device_id=(row, cd, pd), device_id_type=MESH).start()

    final_copy.wait()
    for i in range(6):
        @pl.when(jnp.logical_not((source_of(i) == c) & (i // 2 == p)))
        def _():
            pltpu.make_async_remote_copy(
                src_ref=C.at[0], dst_ref=fin.at[i], send_sem=f_send.at[0], recv_sem=f_recv.at[i],
                device_id=right, device_id_type=MESH).wait_recv()

        keep = qm[0, i].astype(F32)
        masked = xf[i] * xm[i, w_me].astype(F32)
        out[i, 0] = keep * (1.5 * masked - (0.5 * norm) * fin[i].astype(F32))

    for h in range(6):
        x_copy(h).wait_send()
    for d in range(1, 8):
        pm_copy(d).wait_send()
    for i in range(10):
        sib_copy(i, s).wait_send()
    for h in range(1, 5):
        for o in range(3):
            for way in range(2):
                for a in halves(way, h):
                    ring_copy(way, h, a, o, source(way, h)).wait_send()
    for j in range(6):
        @pl.when(jnp.logical_not(targets[j][2]))
        def _():
            pltpu.make_async_remote_copy(
                src_ref=C.at[j], dst_ref=fin.at[0], send_sem=f_send.at[j], recv_sem=f_recv.at[0],
                device_id=right, device_id_type=MESH).wait_send()


def body(x_tiles, x_mask, p_mask, q_mask):
    rows, BW, T = x_tiles.shape[0], x_tiles.shape[1], x_tiles.shape[2]
    n_rows = lax.axis_size("row")
    dma = pltpu.SemaphoreType.DMA

    def run(*refs):
        kernel(T, BW, n_rows, *refs)

    return pl.pallas_call(
        run,
        out_shape=jax.ShapeDtypeStruct((rows, 1, T, T), F32),
        in_specs=[pl.BlockSpec(memory_space=pltpu.SMEM)] * 3 + [pl.BlockSpec(memory_space=pl.ANY)],
        out_specs=pl.BlockSpec(memory_space=pltpu.VMEM),
        scratch_shapes=[
            pltpu.VMEM((6, 6, T, T), F32),
            pltpu.VMEM((4, 6, T, T), F32),
            pltpu.VMEM((2, BW, T, T), F32),
            pltpu.VMEM((6, T, T), F32),
            pltpu.VMEM((6, 6 * T, T), BF16),
            pltpu.VMEM((4, 36 * T, T), BF16),
            pltpu.VMEM((2, T, BW * T), BF16),
            pltpu.VMEM((2, T, BW * T), BF16),
            pltpu.VMEM((8, 8, T), F32),
            pltpu.VMEM((6, T, T), BF16),
            pltpu.VMEM((6, T, T), BF16),
            dma((6,)), dma((4,)), dma, dma, dma((6,)), dma((6,)), dma((10,)), dma((10,)), dma((7,)), dma((7,)),
            dma((2, 4, 6)), dma((2, 4, 6)), dma((6,)), dma((6,)),
        ],
        compiler_params=pltpu.CompilerParams(
            collective_id=0, has_side_effects=True, vmem_limit_bytes=56 * 1024 * 1024),
        name="sign_step",
    )(x_mask, p_mask.T, q_mask.reshape(1, rows), x_tiles)


def solution(mesh):
    in_specs = (
        P("row", None, None, None),
        P("row", None),
        P("row", "col"),
        P("row", ("col", "rep")),
    )
    out_specs = P("row", ("col", "rep"), None, None)
    return jax.shard_map(body, mesh=mesh, in_specs=in_specs, out_specs=out_specs, check_vma=False)
```

time: 72.9 us -> 71.2 us (0.977)
  local copies, waits for them, and re-layouts: 4.44 us -> 1.77 us
  Pallas kernels: 68.3 us -> 69.2 us
    unnamed x3 -> x1, local copies, waits for them, and re-layouts: 4.44 us -> 1.77 us
    pallas_call x1, Pallas kernels: 68.3 us -> 69.2 us  [body(): pl.pallas_call(run, out_shape=jax.ShapeDtypeStruct((rows, 1, T, T), F32),...]
where the time goes in v2:
time: 71.2 us; the launch traced here: 71 us
  Pallas kernels  69.2 us (97%)
  local copies, waits for them, and re-layouts  1.77 us (2%)
    pallas_call x1, Pallas kernels, body(): pl.pallas_call(run, out_shape=jax.ShapeDtypeStruct((rows, 1, T, T), F32),...  69.2 us
    unnamed x1, local copies, waits for them, and re-layouts  1.77 us

profile of v2, /device:TPU:1, one launch (start us, length us, event | category | flops | bytes accessed | tf_op | source)
XLA Modules:
  0.0 71.0 jit_solution(8653664959796345160)
XLA Ops:
  0.0 69.2 %sign_step.1 = f32[6,1,128,128]{3,2,1,0:T(8,128)} custom-call(s32[6,24]{1,0:T(8,128)} %refs_0_.1, s32[3,6]{1,0:T(4,128)} %bitcast.2, s32[1,6]{1,0:T(1,128)} %bitcast.3, f32[6,24,128,128]{3,2,1,0:T(8,128)} %refs_3_.1), custom_call_target="tpu_custom_call" | custom-call | tf_op jit(solution)/shard_map/sign_step/pallas_call | solution.py:284
  69.2 1.8 %copy.6 = f32[6,1,128,128]{3,2,1,0:T(8,128)} copy(f32[6,1,128,128]{3,2,1,0:T(8,128)} %sign_step.1) | data formatting | bytes 786432

commit v3 on v2

--- a/solution.py
+++ b/solution.py
@@ -12,7 +12,7 @@
 
 
 def kernel(T, BW, n_rows, xm, pm, qm, x_hbm, out, xs, xo, xl, xf, S, R, L, Q, PM, C, fin,
-           ls_sem, lo_sem, ll_sem, lf_sem, x_send, x_recv, sib_send, sib_recv, pm_send, pm_recv,
+           ls_sem, lo_sem, ll_sem, lf_sem, x_send, x_recv, sib_send, sib_recv, pass_send, pass_recv, pm_send, pm_recv,
            r_send, r_recv, f_send, f_recv):
     row, c, p = lax.axis_index("row"), lax.axis_index("col"), lax.axis_index("rep")
     n_chip = n_rows // 2
@@ -24,12 +24,25 @@
     fwd = (lax.rem(row + 2, n_rows), c, p_fwd)
     bwd = (lax.rem(row + n_rows - 2, n_rows), c, p_bwd)
     sib = (row + 1 - 2 * s, c, p)
-    right = (row, lax.rem(c + 1, 8), p)
-    left = (row, lax.rem(c + 7, 8), p)
+
+    def beside(d):
+        return (row, lax.rem(c + 8 + d, 8), p)
+
     w_me = 3 * c + p
 
+    def base_of(h, rep, core):
+        return (2 * rep + 12 + 8 * h if h < 3 else 2 * rep - 12 + 8 * (h - 2)) + c - 6 * core
+
+    def needed(h, k, rep, core):
+        w = base_of(h, rep, core) - k
+        near = 6 * core + k >= 2 * rep if h < 3 else 6 * core + k <= 6 + 2 * rep
+        return (w >= 0) & (w < BW) & near
+
+    def halo_rep(h):
+        return p_fwd if h < 3 else p_bwd
+
     def halo_base(h):
-        return (2 * p_fwd + 12 + 8 * h if h < 3 else 2 * p_bwd - 12 + 8 * (h - 2)) + c - 6 * s
+        return base_of(h, halo_rep(h), s)
 
     def own_base(m):
         return 2 * p + c - 6 * s + 8 * m
@@ -96,7 +109,9 @@
 
         @pl.loop(0, 6)
         def _(k):
-            S[h, pl.ds(pl.multiple_of(k * T, T), T), :] = (xs[h, k] * scale_of(k, base - k)).astype(BF16)
+            @pl.when(needed(h, k, halo_rep(h), s))
+            def _():
+                S[h, pl.ds(pl.multiple_of(k * T, T), T), :] = (xs[h, k] * scale_of(k, base - k)).astype(BF16)
 
     def make_own(m):
         base = own_base(m)
@@ -107,35 +122,55 @@
             at = pl.multiple_of((12 + 6 * s + k) * T, T)
             R[m, pl.ds(at, T), :] = (xo[m, k] * scale_of(k, base - k)).astype(BF16)
 
-    def x_copy(h):
-        m = h if h < 3 else h - 2
-        place = (0 if h < 3 else 24) + 6 * s
-        return pltpu.make_async_remote_copy(
-            src_ref=S.at[h], dst_ref=R.at[m, pl.ds(pl.multiple_of(place * T, T), 6 * T)],
-            send_sem=x_send.at[h], recv_sem=x_recv.at[h],
+    def part_of(h, k, core):
+        m, place = (h, 0) if h < 3 else (h - 2, 24)
+        return R.at[m, pl.ds(pl.multiple_of((place + 6 * core + k) * T, T), T)]
+
+    def x_copy(h, k):
+        return pltpu.make_async_remote_copy(
+            src_ref=S.at[h, pl.ds(pl.multiple_of(k * T, T), T)], dst_ref=part_of(h, k, s),
+            send_sem=x_send.at[h, k], recv_sem=x_recv.at[h, k],
             device_id=fwd if h < 3 else bwd, device_id_type=MESH)
+
+    def each(h, rep, core, do, other=None):
+        @pl.loop(0, 6)
+        def _(k):
+            need = needed(h, k, rep, core)
+
+            @pl.when(need)
+            def _():
+                do(k)
+
+            if other is not None:
+                @pl.when(jnp.logical_not(need))
+                def _():
+                    other(k)
+
+    def x_start(h):
+        each(h, halo_rep(h), s, lambda k: x_copy(h, k).start())
 
     def pm_copy(d):
         return pltpu.make_async_remote_copy(
             src_ref=PM.at[c], dst_ref=PM.at[c], send_sem=pm_send.at[d - 1], recv_sem=pm_recv.at[d - 1],
             device_id=(row, lax.rem(c + d, 8), p), device_id_type=MESH)
 
-    def sib_copy(i, half):
-        if i < 4:
-            m, place = i, 12
-        else:
-            h = i - 4
-            m, place = (h, 0) if h < 3 else (h - 2, 24)
-        part = R.at[m, pl.ds(pl.multiple_of((place + 6 * half) * T, T), 6 * T)]
-        return pltpu.make_async_remote_copy(
-            src_ref=part, dst_ref=part, send_sem=sib_send.at[i], recv_sem=sib_recv.at[i],
+    def sib_copy(m, core):
+        part = R.at[m, pl.ds(pl.multiple_of((12 + 6 * core) * T, T), 6 * T)]
+        return pltpu.make_async_remote_copy(
+            src_ref=part, dst_ref=part, send_sem=sib_send.at[m], recv_sem=sib_recv.at[m],
+            device_id=sib, device_id_type=MESH)
+
+    def pass_copy(h, k, core):
+        part = part_of(h, k, core)
+        return pltpu.make_async_remote_copy(
+            src_ref=part, dst_ref=part, send_sem=pass_send.at[h, k], recv_sem=pass_recv.at[h, k],
             device_id=sib, device_id_type=MESH)
 
     make_halo(1)
     make_halo(3)
     pl.semaphore_wait(barrier, 10 + n_out)
-    x_copy(1).start()
-    x_copy(3).start()
+    x_start(1)
+    x_start(3)
     PM[c] = jnp.zeros((8, T), F32)
     for wl in range(3):
         for a in range(2):
@@ -144,12 +179,12 @@
         pm_copy(d).start()
     for h in (2, 4):
         make_halo(h)
-        x_copy(h).start()
+        x_start(h)
     make_own(1)
     sib_copy(1, s).start()
     for h in (0, 5):
         make_halo(h)
-        x_copy(h).start()
+        x_start(h)
     rows_copy.wait()
 
     @pl.loop(0, BW)
@@ -162,6 +197,12 @@
         sib_copy(m, s).start()
     R[3, pl.ds(0, 12 * T), :] = jnp.zeros((12 * T, T), BF16)
     R[0, pl.ds(24 * T, 12 * T), :] = jnp.zeros((12 * T, T), BF16)
+    for h in range(6):
+        for core in range(2):
+            def clear(k):
+                part_of(h, k, core)[...] = jnp.zeros((T, T), BF16)
+
+            each(h, p, core, lambda k: None, clear)
 
     for d in range(1, 8):
         pm_copy(d).wait_recv()
@@ -180,12 +221,13 @@
         w, _ = place_of(src, a, o)
         part = Q.at[a, :, pl.ds(pl.multiple_of(w * T, T), T)]
         j = a * 3 + o
+        d = 1 if h in (1, 3) else 2
         return pltpu.make_async_remote_copy(
             src_ref=part, dst_ref=part, send_sem=r_send.at[way, h - 1, j], recv_sem=r_recv.at[way, h - 1, j],
-            device_id=right if way == 0 else left, device_id_type=MESH)
-
-    def source(way, h):
-        return lax.rem(c + 8 - (h - 1), 8) if way == 0 else lax.rem(c + h - 1, 8)
+            device_id=beside(d if way == 0 else -d), device_id_type=MESH)
+
+    def origin(way, h):
+        return lax.rem(c + 8 - h if way == 0 else c + h, 8)
 
     def halves(way, h):
         return (0, 1) if h < 4 else (way,)
@@ -193,35 +235,44 @@
     def square_round(o):
         hs, ms = (((1, 3), (1,)), ((2, 4), (2,)), ((0, 5), (0, 3)))[o]
         for h in hs:
-            x_copy(h).wait_recv()
-            sib_copy(4 + h, s).start()
+            def forward(k):
+                x_copy(h, k).wait_recv()
+                pass_copy(h, k, s).start()
+
+            each(h, p, s, forward)
         for m in ms:
             sib_copy(m, 1 - s).wait_recv()
         for h in hs:
-            sib_copy(4 + h, 1 - s).wait_recv()
+            each(h, p, 1 - s, lambda k: pass_copy(h, k, 1 - s).wait_recv())
         for a in range(2):
             w, m = place_of(c, a, o)
             acc = jnp.dot(L[a], column(a, m), preferred_element_type=F32)
             keep = PM[lax.div(w, 3), pl.ds(lax.rem(w, 3) * 2 + a, 1), :]
             Q[a, :, pl.ds(pl.multiple_of(w * T, T), T)] = (acc * keep).astype(BF16)
+            for h in (2, 1):
+                for way in range(2):
+                    ring_copy(way, h, a, o, c).start()
+
+    def ring_forward(o):
+        for a in range(2):
             for way in range(2):
-                ring_copy(way, 1, a, o, source(way, 1)).start()
-
-    def ring_step(h, o):
-        for way in range(2):
-            for a in halves(way, h):
-                ring_copy(way, h, a, o, source(way, h + 1)).wait_recv()
-                if h < 4 and a in halves(way, h + 1):
-                    ring_copy(way, h + 1, a, o, source(way, h + 1)).start()
+                src = origin(way, 2)
+                ring_copy(way, 2, a, o, src).wait_recv()
+                if a == way:
+                    ring_copy(way, 4, a, o, src).start()
+                ring_copy(way, 3, a, o, src).start()
 
     square_round(0)
-    ring_step(1, 0)
     square_round(1)
-    ring_step(2, 0)
-    ring_step(1, 1)
+    ring_forward(0)
     square_round(2)
-    for h, o in ((3, 0), (2, 1), (1, 2), (4, 0), (3, 1), (2, 2), (4, 1), (3, 2), (4, 2)):
-        ring_step(h, o)
+    ring_forward(1)
+    ring_forward(2)
+    for o in range(3):
+        for h in (1, 3, 4):
+            for way in range(2):
+                for a in halves(way, h):
+                    ring_copy(way, h, a, o, origin(way, h)).wait_recv()
 
     for a in range(2):
         for e in range(3):
@@ -248,29 +299,30 @@
         def _():
             pltpu.make_async_remote_copy(
                 src_ref=C.at[0], dst_ref=fin.at[i], send_sem=f_send.at[0], recv_sem=f_recv.at[i],
-                device_id=right, device_id_type=MESH).wait_recv()
+                device_id=beside(1), device_id_type=MESH).wait_recv()
 
         keep = qm[0, i].astype(F32)
         masked = xf[i] * xm[i, w_me].astype(F32)
         out[i, 0] = keep * (1.5 * masked - (0.5 * norm) * fin[i].astype(F32))
 
     for h in range(6):
-        x_copy(h).wait_send()
+        each(h, halo_rep(h), s, lambda k: x_copy(h, k).wait_send())
+        each(h, p, s, lambda k: pass_copy(h, k, s).wait_send())
     for d in range(1, 8):
         pm_copy(d).wait_send()
-    for i in range(10):
-        sib_copy(i, s).wait_send()
+    for m in range(4):
+        sib_copy(m, s).wait_send()
     for h in range(1, 5):
         for o in range(3):
             for way in range(2):
                 for a in halves(way, h):
-                    ring_copy(way, h, a, o, source(way, h)).wait_send()
+                    ring_copy(way, h, a, o, c).wait_send()
     for j in range(6):
         @pl.when(jnp.logical_not(targets[j][2]))
         def _():
             pltpu.make_async_remote_copy(
                 src_ref=C.at[j], dst_ref=fin.at[0], send_sem=f_send.at[j], recv_sem=f_recv.at[0],
-                device_id=right, device_id_type=MESH).wait_send()
+                device_id=beside(1), device_id_type=MESH).wait_send()
 
 
 def body(x_tiles, x_mask, p_mask, q_mask):
@@ -298,7 +350,8 @@
             pltpu.VMEM((8, 8, T), F32),
             pltpu.VMEM((6, T, T), BF16),
             pltpu.VMEM((6, T, T), BF16),
-            dma((6,)), dma((4,)), dma, dma, dma((6,)), dma((6,)), dma((10,)), dma((10,)), dma((7,)), dma((7,)),
+            dma((6,)), dma((4,)), dma, dma, dma((6, 6)), dma((6, 6)), dma((4,)), dma((4,)), dma((6, 6)), dma((6, 6)),
+            dma((7,)), dma((7,)),
             dma((2, 4, 6)), dma((2, 4, 6)), dma((6,)), dma((6,)),
         ],
         compiler_params=pltpu.CompilerParams(

time: 71.2 us -> 70 us (0.983)
  Pallas kernels: 69.2 us -> 68 us
    pallas_call x1, Pallas kernels: 69.2 us -> 68 us  [body(): pl.pallas_call(run, out_shape=jax.ShapeDtypeStruct((rows, 1, T, T), F32),...]
where the time goes in v3:
time: 70 us; the launch traced here: 69.8 us
  Pallas kernels  68 us (97%)
  local copies, waits for them, and re-layouts  1.77 us (3%)
    pallas_call x1, Pallas kernels, body(): pl.pallas_call(run, out_shape=jax.ShapeDtypeStruct((rows, 1, T, T), F32),...  68 us
    unnamed x1, local copies, waits for them, and re-layouts  1.77 us

profile of v3, /device:TPU:1, one launch (start us, length us, event | category | flops | bytes accessed | tf_op | source)
XLA Modules:
  0.0 69.8 jit_solution(9792838760484303577)
XLA Ops:
  0.0 68.0 %sign_step.1 = f32[6,1,128,128]{3,2,1,0:T(8,128)} custom-call(s32[6,24]{1,0:T(8,128)} %refs_0_.1, s32[3,6]{1,0:T(4,128)} %bitcast.2, s32[1,6]{1,0:T(1,128)} %bitcast.3, f32[6,24,128,128]{3,2,1,0:T(8,128)} %refs_3_.1), custom_call_target="tpu_custom_call" | custom-call | tf_op jit(solution)/shard_map/sign_step/pallas_call | solution.py:336
  68.0 1.8 %copy.6 = f32[6,1,128,128]{3,2,1,0:T(8,128)} copy(f32[6,1,128,128]{3,2,1,0:T(8,128)} %sign_step.1) | data formatting | bytes 786432

commit v4 on v2

--- a/solution.py
+++ b/solution.py
@@ -11,9 +11,9 @@
 F32, BF16 = jnp.float32, jnp.bfloat16
 
 
-def kernel(T, BW, n_rows, xm, pm, qm, x_hbm, out, xs, xo, xl, xf, S, R, L, Q, PM, C, fin,
-           ls_sem, lo_sem, ll_sem, lf_sem, x_send, x_recv, sib_send, sib_recv, pm_send, pm_recv,
-           r_send, r_recv, f_send, f_recv):
+def kernel(T, BW, n_rows, xm, pm, qm, x_hbm, out, xs, xo, xl, xf, S, R, L, Q, PM, C, fin, ob,
+           ls_sem, lo_sem, ll_sem, lf_sem, x_send, x_recv, sib_send, sib_recv, pass_send, pass_recv,
+           pm_send, pm_recv, r_send, r_recv, f_send, f_recv, o_sem):
     row, c, p = lax.axis_index("row"), lax.axis_index("col"), lax.axis_index("rep")
     n_chip = n_rows // 2
     q, s = lax.div(row, 2), lax.rem(row, 2)
@@ -21,12 +21,43 @@
     inv_norm = 1.0 / norm
     p_fwd = jnp.where(q == n_chip - 1, lax.rem(p + 1, 3), p)
     p_bwd = jnp.where(q == 0, lax.rem(p + 2, 3), p)
-    fwd = (lax.rem(row + 2, n_rows), c, p_fwd)
-    bwd = (lax.rem(row + n_rows - 2, n_rows), c, p_bwd)
+
+    def fwd(core):
+        return (2 * lax.rem(q + 1, n_chip) + core, c, p_fwd)
+
+    def bwd(core):
+        return (2 * lax.rem(q + n_chip - 1, n_chip) + core, c, p_bwd)
+
     sib = (row + 1 - 2 * s, c, p)
     right = (row, lax.rem(c + 1, 8), p)
     left = (row, lax.rem(c + 7, 8), p)
     w_me = 3 * c + p
+
+    def halo_rep(h):
+        return p_fwd if h < 3 else p_bwd
+
+    def needed(h, rep, core):
+        v = c + 2 * rep
+        return (None, v <= 8 + 6 * core, v <= 6 * core, v >= 4 + 6 * core, v >= 2 * core, c <= 6)[h]
+
+    def on(h, rep, core, do):
+        need = needed(h, rep, core)
+        if need is None:
+            do(0, 6)
+        elif h in (2, 3):
+            few = 0 if h == 2 else 1
+
+            @pl.when(need & (core != few))
+            def _():
+                do(0, 6)
+
+            @pl.when(need & (core == few))
+            def _():
+                do(*((5, 1) if h == 2 else (0, 2)))
+        else:
+            @pl.when(need)
+            def _():
+                do(0, 6)
 
     def halo_base(h):
         return (2 * p_fwd + 12 + 8 * h if h < 3 else 2 * p_bwd - 12 + 8 * (h - 2)) + c - 6 * s
@@ -61,7 +92,7 @@
         return lax.rem(lax.rem(src + 2 * s, 8) + 8 - a, 8)
 
     barrier = pltpu.get_barrier_semaphore()
-    for peer in (fwd, bwd, sib):
+    for peer in (fwd(0), fwd(1), bwd(0), bwd(1), sib):
         pl.semaphore_signal(barrier, inc=1, device_id=peer, device_id_type=MESH)
     for d in range(1, 8):
         pl.semaphore_signal(barrier, inc=1, device_id=(row, lax.rem(c + d, 8), p), device_id_type=MESH)
@@ -78,12 +109,15 @@
 
     targets = []
     n_out = jnp.int32(0)
+    m_first = [lax.div(first_of(c, a) + a + 6 * s - c, 8) for a in range(2)]
     for a in range(2):
-        for e in range(3):
+        e_last = lax.rem(2 * (p + 24 - first_of(c, a)), 3)
+        for i in range(3):
+            e = lax.rem(e_last + 1 + i, 3)
             w = first_of(c, a) + 8 * e
             cd, pd = lax.div(w, 3), lax.rem(w, 3)
             own = (cd == c) & (pd == p)
-            targets.append((cd, pd, own))
+            targets.append((e, cd, pd, own))
             n_out = n_out + jnp.where(own, 0, 1)
 
     def scale_of(k, w):
@@ -107,35 +141,42 @@
             at = pl.multiple_of((12 + 6 * s + k) * T, T)
             R[m, pl.ds(at, T), :] = (xo[m, k] * scale_of(k, base - k)).astype(BF16)
 
-    def x_copy(h):
-        m = h if h < 3 else h - 2
-        place = (0 if h < 3 else 24) + 6 * s
+    def part_of(h, core, k, n):
+        m, place = (h, 0) if h < 3 else (h - 2, 24)
+        return R.at[m, pl.ds(pl.multiple_of((place + 6 * core + k) * T, T), n * T)]
+
+    def x_copy(h, core, k, n):
+        to = 0 if h == 0 else 1 if h == 5 else s
         return pltpu.make_async_remote_copy(
-            src_ref=S.at[h], dst_ref=R.at[m, pl.ds(pl.multiple_of(place * T, T), 6 * T)],
-            send_sem=x_send.at[h], recv_sem=x_recv.at[h],
-            device_id=fwd if h < 3 else bwd, device_id_type=MESH)
+            src_ref=S.at[h, pl.ds(k * T, n * T)], dst_ref=part_of(h, core, k, n),
+            send_sem=x_send.at[h], recv_sem=x_recv.at[h, core],
+            device_id=fwd(to) if h < 3 else bwd(to), device_id_type=MESH)
+
+    def x_start(h):
+        on(h, halo_rep(h), s, lambda k, n: x_copy(h, s, k, n).start())
+
+    def pass_copy(h, core, k, n):
+        part = part_of(h, core, k, n)
+        return pltpu.make_async_remote_copy(
+            src_ref=part, dst_ref=part, send_sem=pass_send.at[h, core], recv_sem=pass_recv.at[h, core],
+            device_id=sib, device_id_type=MESH)
 
     def pm_copy(d):
         return pltpu.make_async_remote_copy(
             src_ref=PM.at[c], dst_ref=PM.at[c], send_sem=pm_send.at[d - 1], recv_sem=pm_recv.at[d - 1],
             device_id=(row, lax.rem(c + d, 8), p), device_id_type=MESH)
 
-    def sib_copy(i, half):
-        if i < 4:
-            m, place = i, 12
-        else:
-            h = i - 4
-            m, place = (h, 0) if h < 3 else (h - 2, 24)
-        part = R.at[m, pl.ds(pl.multiple_of((place + 6 * half) * T, T), 6 * T)]
+    def sib_copy(m, core):
+        part = R.at[m, pl.ds(pl.multiple_of((12 + 6 * core) * T, T), 6 * T)]
         return pltpu.make_async_remote_copy(
-            src_ref=part, dst_ref=part, send_sem=sib_send.at[i], recv_sem=sib_recv.at[i],
+            src_ref=part, dst_ref=part, send_sem=sib_send.at[m], recv_sem=sib_recv.at[m],
             device_id=sib, device_id_type=MESH)
 
     make_halo(1)
     make_halo(3)
-    pl.semaphore_wait(barrier, 10 + n_out)
-    x_copy(1).start()
-    x_copy(3).start()
+    pl.semaphore_wait(barrier, 12 + n_out)
+    x_start(1)
+    x_start(3)
     PM[c] = jnp.zeros((8, T), F32)
     for wl in range(3):
         for a in range(2):
@@ -144,12 +185,12 @@
         pm_copy(d).start()
     for h in (2, 4):
         make_halo(h)
-        x_copy(h).start()
+        x_start(h)
     make_own(1)
     sib_copy(1, s).start()
     for h in (0, 5):
         make_halo(h)
-        x_copy(h).start()
+        x_start(h)
     rows_copy.wait()
 
     @pl.loop(0, BW)
@@ -162,6 +203,15 @@
         sib_copy(m, s).start()
     R[3, pl.ds(0, 12 * T), :] = jnp.zeros((12 * T, T), BF16)
     R[0, pl.ds(24 * T, 12 * T), :] = jnp.zeros((12 * T, T), BF16)
+    R[2, pl.ds(0, 5 * T), :] = jnp.zeros((5 * T, T), BF16)
+    R[1, pl.ds(32 * T, 4 * T), :] = jnp.zeros((4 * T, T), BF16)
+    for h in range(1, 5):
+        for core in range(2):
+            k, n = (5, 1) if (h, core) == (2, 0) else (0, 2) if (h, core) == (3, 1) else (0, 6)
+
+            @pl.when(jnp.logical_not(needed(h, p, core)))
+            def _():
+                part_of(h, core, k, n)[...] = jnp.zeros((n * T, T), BF16)
 
     for d in range(1, 8):
         pm_copy(d).wait_recv()
@@ -190,15 +240,46 @@
     def halves(way, h):
         return (0, 1) if h < 4 else (way,)
 
+    def halo_round(o):
+        hs, m = (((1, 3), 1), ((2, 4), 2))[o]
+        for h in hs:
+            def forward(k, n):
+                x_copy(h, s, k, n).wait_recv()
+                pass_copy(h, s, k, n).start()
+
+            on(h, p, s, forward)
+        sib_copy(m, 1 - s).wait_recv()
+        for h in hs:
+            on(h, p, 1 - s, lambda k, n: pass_copy(h, 1 - s, k, n).wait_recv())
+
+    both0, both3 = c >= 6, c == 0
+
+    def last_round():
+        for h, core, use, both in ((0, 0, None, both0), (5, 1, c <= 6, both3)):
+            mine = s == core
+
+            @pl.when(mine if use is None else mine & use)
+            def _():
+                for half in (1, 0):
+                    x_copy(h, half, 0, 6).wait_recv()
+
+                    @pl.when(both)
+                    def _():
+                        pass_copy(h, half, 0, 6).start()
+
+        for m in (0, 3):
+            sib_copy(m, 1 - s).wait_recv()
+        for h, core, both in ((0, 0, both0), (5, 1, both3)):
+            @pl.when((s != core) & both)
+            def _():
+                for half in (1, 0):
+                    pass_copy(h, half, 0, 6).wait_recv()
+
     def square_round(o):
-        hs, ms = (((1, 3), (1,)), ((2, 4), (2,)), ((0, 5), (0, 3)))[o]
-        for h in hs:
-            x_copy(h).wait_recv()
-            sib_copy(4 + h, s).start()
-        for m in ms:
-            sib_copy(m, 1 - s).wait_recv()
-        for h in hs:
-            sib_copy(4 + h, 1 - s).wait_recv()
+        if o < 2:
+            halo_round(o)
+        else:
+            last_round()
         for a in range(2):
             w, m = place_of(c, a, o)
             acc = jnp.dot(L[a], column(a, m), preferred_element_type=F32)
@@ -218,18 +299,15 @@
     ring_step(1, 0)
     square_round(1)
     ring_step(2, 0)
-    ring_step(1, 1)
     square_round(2)
-    for h, o in ((3, 0), (2, 1), (1, 2), (4, 0), (3, 1), (2, 2), (4, 1), (3, 2), (4, 2)):
+    for h, o in ((1, 1), (1, 2), (2, 1), (3, 0), (2, 2), (4, 0), (3, 1), (3, 2), (4, 1), (4, 2)):
         ring_step(h, o)
 
-    for a in range(2):
-        for e in range(3):
-            j = a * 3 + e
-            cd, pd, own = targets[j]
-            w0 = first_of(c, a)
-            m = lax.div(w0 + a + 6 * s - c, 8) + e
-            value = jnp.dot(Q[a], column(a, m), preferred_element_type=F32).astype(BF16)
+    for i in range(3):
+        for a in range(2):
+            j = 3 * a + i
+            e, cd, pd, own = targets[j]
+            value = jnp.dot(Q[a], column(a, m_first[a] + e), preferred_element_type=F32).astype(BF16)
             C[j] = value
 
             @pl.when(own)
@@ -241,6 +319,9 @@
                 pltpu.make_async_remote_copy(
                     src_ref=C.at[j], dst_ref=fin.at[2 * p + a], send_sem=f_send.at[j],
                     recv_sem=f_recv.at[2 * p + a], device_id=(row, cd, pd), device_id_type=MESH).start()
+
+    def out_copy(i):
+        return pltpu.make_async_copy(ob.at[i], out.at[i, 0], o_sem.at[i])
 
     final_copy.wait()
     for i in range(6):
@@ -252,25 +333,35 @@
 
         keep = qm[0, i].astype(F32)
         masked = xf[i] * xm[i, w_me].astype(F32)
-        out[i, 0] = keep * (1.5 * masked - (0.5 * norm) * fin[i].astype(F32))
+        ob[i] = keep * (1.5 * masked - (0.5 * norm) * fin[i].astype(F32))
+        out_copy(i).start()
 
     for h in range(6):
-        x_copy(h).wait_send()
+        on(h, halo_rep(h), s, lambda k, n: x_copy(h, s, k, n).wait_send())
+    for h in range(1, 5):
+        on(h, p, s, lambda k, n: pass_copy(h, s, k, n).wait_send())
+    for h, core, both in ((0, 0, both0), (5, 1, both3)):
+        @pl.when((s == core) & both)
+        def _():
+            for half in range(2):
+                pass_copy(h, half, 0, 6).wait_send()
     for d in range(1, 8):
         pm_copy(d).wait_send()
-    for i in range(10):
-        sib_copy(i, s).wait_send()
+    for m in range(4):
+        sib_copy(m, s).wait_send()
     for h in range(1, 5):
         for o in range(3):
             for way in range(2):
                 for a in halves(way, h):
                     ring_copy(way, h, a, o, source(way, h)).wait_send()
     for j in range(6):
-        @pl.when(jnp.logical_not(targets[j][2]))
+        @pl.when(jnp.logical_not(targets[j][3]))
         def _():
             pltpu.make_async_remote_copy(
                 src_ref=C.at[j], dst_ref=fin.at[0], send_sem=f_send.at[j], recv_sem=f_recv.at[0],
                 device_id=right, device_id_type=MESH).wait_send()
+    for i in range(6):
+        out_copy(i).wait()
 
 
 def body(x_tiles, x_mask, p_mask, q_mask):
@@ -285,7 +376,7 @@
         run,
         out_shape=jax.ShapeDtypeStruct((rows, 1, T, T), F32),
         in_specs=[pl.BlockSpec(memory_space=pltpu.SMEM)] * 3 + [pl.BlockSpec(memory_space=pl.ANY)],
-        out_specs=pl.BlockSpec(memory_space=pltpu.VMEM),
+        out_specs=pl.BlockSpec(memory_space=pl.ANY),
         scratch_shapes=[
             pltpu.VMEM((6, 6, T, T), F32),
             pltpu.VMEM((4, 6, T, T), F32),
@@ -298,8 +389,10 @@
             pltpu.VMEM((8, 8, T), F32),
             pltpu.VMEM((6, T, T), BF16),
             pltpu.VMEM((6, T, T), BF16),
-            dma((6,)), dma((4,)), dma, dma, dma((6,)), dma((6,)), dma((10,)), dma((10,)), dma((7,)), dma((7,)),
-            dma((2, 4, 6)), dma((2, 4, 6)), dma((6,)), dma((6,)),
+            pltpu.VMEM((6, T, T), F32),
+            dma((6,)), dma((4,)), dma, dma, dma((6,)), dma((6, 2)), dma((4,)), dma((4,)), dma((6, 2)), dma((6, 2)),
+            dma((7,)), dma((7,)),
+            dma((2, 4, 6)), dma((2, 4, 6)), dma((6,)), dma((6,)), dma((6,)),
         ],
         compiler_params=pltpu.CompilerParams(
             collective_id=0, has_side_effects=True, vmem_limit_bytes=56 * 1024 * 1024),

time: 71.2 us -> 68.7 us (0.965)
  Pallas kernels: 69.2 us -> 66.7 us
    pallas_call x1, Pallas kernels: 69.2 us -> 66.7 us  [body(): pl.pallas_call(run, out_shape=jax.ShapeDtypeStruct((rows, 1, T, T), F32),...]
where the time goes in v4:
time: 68.7 us; the launch traced here: 68.5 us
  Pallas kernels  66.7 us (97%)
  local copies, waits for them, and re-layouts  1.77 us (3%)
    pallas_call x1, Pallas kernels, body(): pl.pallas_call(run, out_shape=jax.ShapeDtypeStruct((rows, 1, T, T), F32),...  66.7 us
    unnamed x1, local copies, waits for them, and re-layouts  1.77 us

profile of v4, /device:TPU:1, one launch (start us, length us, event | category | flops | bytes accessed | tf_op | source)
XLA Modules:
  0.0 68.5 jit_solution(16399353334344025868)
XLA Ops:
  0.0 66.7 %sign_step.1 = f32[6,1,128,128]{3,2,1,0:T(8,128)} custom-call(s32[6,24]{1,0:T(8,128)} %refs_0_.1, s32[3,6]{1,0:T(4,128)} %bitcast.2, s32[1,6]{1,0:T(1,128)} %bitcast.3, f32[6,24,128,128]{3,2,1,0:T(8,128)} %refs_3_.1), custom_call_target="tpu_custom_call" | custom-call | tf_op jit(solution)/shard_map/sign_step/pallas_call | solution.py:375
  66.7 1.8 %copy.6 = f32[6,1,128,128]{3,2,1,0:T(8,128)} copy(f32[6,1,128,128]{3,2,1,0:T(8,128)} %sign_step.1) | data formatting | bytes 786432

commit v5 on v4

--- a/solution.py
+++ b/solution.py
@@ -295,13 +295,11 @@
                 if h < 4 and a in halves(way, h + 1):
                     ring_copy(way, h + 1, a, o, source(way, h + 1)).start()
 
-    square_round(0)
-    ring_step(1, 0)
-    square_round(1)
-    ring_step(2, 0)
-    square_round(2)
-    for h, o in ((1, 1), (1, 2), (2, 1), (3, 0), (2, 2), (4, 0), (3, 1), (3, 2), (4, 1), (4, 2)):
-        ring_step(h, o)
+    for o in range(3):
+        square_round(o)
+    for h in range(1, 5):
+        for o in range(3):
+            ring_step(h, o)
 
     for i in range(3):
         for a in range(2):

time: 68.7 us -> 65 us (0.946)
  the two profiles are of different devices: /device:TPU:1 before, /device:TPU:8 now
where the time goes in v5:
time: 65 us; the launch traced here: 64.8 us
  Pallas kernels  63 us (97%)
  local copies, waits for them, and re-layouts  1.77 us (3%)
    pallas_call x1, Pallas kernels, body(): pl.pallas_call(run, out_shape=jax.ShapeDtypeStruct((rows, 1, T, T), F32),...  63 us
    unnamed x1, local copies, waits for them, and re-layouts  1.77 us

profile of v5, /device:TPU:8, one launch (start us, length us, event | category | flops | bytes accessed | tf_op | source)
XLA Modules:
  0.0 64.8 jit_solution(9783875960532680101)
XLA Ops:
  0.0 63.0 %sign_step.1 = f32[6,1,128,128]{3,2,1,0:T(8,128)} custom-call(s32[6,24]{1,0:T(8,128)} %refs_0_.1, s32[3,6]{1,0:T(4,128)} %bitcast.2, s32[1,6]{1,0:T(1,128)} %bitcast.3, f32[6,24,128,128]{3,2,1,0:T(8,128)} %refs_3_.1), custom_call_target="tpu_custom_call" | custom-call | tf_op jit(solution)/shard_map/sign_step/pallas_call | solution.py:373
  63.0 1.8 %copy.6 = f32[6,1,128,128]{3,2,1,0:T(8,128)} copy(f32[6,1,128,128]{3,2,1,0:T(8,128)} %sign_step.1) | data formatting | bytes 786432

commit v6 on v5

--- a/solution.py
+++ b/solution.py
@@ -72,21 +72,6 @@
 
     def loaded(buf, sem):
         pltpu.make_async_copy(x_hbm.at[pl.ds(0, 6), 0], buf, sem).wait()
-
-    for h in (1, 3):
-        load(halo_base(h), xs.at[h], ls_sem.at[h])
-    load(own_base(1), xo.at[1], lo_sem.at[1])
-    for h in (2, 4):
-        load(halo_base(h), xs.at[h], ls_sem.at[h])
-    rows_copy = pltpu.make_async_copy(x_hbm.at[pl.ds(2 * p, 2)], xl, ll_sem)
-    rows_copy.start()
-    load(own_base(2), xo.at[2], lo_sem.at[2])
-    for h in (0, 5):
-        load(halo_base(h), xs.at[h], ls_sem.at[h])
-    for m in (0, 3):
-        load(own_base(m), xo.at[m], lo_sem.at[m])
-    final_copy = pltpu.make_async_copy(x_hbm.at[pl.ds(0, 6), w_me], xf, lf_sem)
-    final_copy.start()
 
     def first_of(src, a):
         return lax.rem(lax.rem(src + 2 * s, 8) + 8 - a, 8)
@@ -120,6 +105,9 @@
             targets.append((e, cd, pd, own))
             n_out = n_out + jnp.where(own, 0, 1)
 
+    for h in (1, 3, 2, 4):
+        load(halo_base(h), xs.at[h], ls_sem.at[h])
+
     def scale_of(k, w):
         ok = (w >= 0) & (w < BW)
         return jnp.where(ok, xm[k, jnp.clip(w, 0, BW - 1)].astype(F32) * inv_norm, 0.0)
@@ -177,6 +165,15 @@
     pl.semaphore_wait(barrier, 12 + n_out)
     x_start(1)
     x_start(3)
+    for h in (0, 5):
+        load(halo_base(h), xs.at[h], ls_sem.at[h])
+    load(own_base(1), xo.at[1], lo_sem.at[1])
+    rows_copy = pltpu.make_async_copy(x_hbm.at[pl.ds(2 * p, 2)], xl, ll_sem)
+    rows_copy.start()
+    for m in (2, 0, 3):
+        load(own_base(m), xo.at[m], lo_sem.at[m])
+    final_copy = pltpu.make_async_copy(x_hbm.at[pl.ds(0, 6), w_me], xf, lf_sem)
+    final_copy.start()
     PM[c] = jnp.zeros((8, T), F32)
     for wl in range(3):
         for a in range(2):
@@ -288,21 +285,18 @@
             for way in range(2):
                 ring_copy(way, 1, a, o, source(way, 1)).start()
 
-    def ring_step(h, o):
-        for way in range(2):
-            for a in halves(way, h):
-                ring_copy(way, h, a, o, source(way, h + 1)).wait_recv()
-                if h < 4 and a in halves(way, h + 1):
-                    ring_copy(way, h + 1, a, o, source(way, h + 1)).start()
+    def ring_step(h, a):
+        for o in range(3):
+            for way in range(2):
+                if a in halves(way, h):
+                    ring_copy(way, h, a, o, source(way, h + 1)).wait_recv()
+                    if h < 4 and a in halves(way, h + 1):
+                        ring_copy(way, h + 1, a, o, source(way, h + 1)).start()
 
     for o in range(3):
         square_round(o)
-    for h in range(1, 5):
-        for o in range(3):
-            ring_step(h, o)
-
-    for i in range(3):
-        for a in range(2):
+    def cube_row(a):
+        for i in range(3):
             j = 3 * a + i
             e, cd, pd, own = targets[j]
             value = jnp.dot(Q[a], column(a, m_first[a] + e), preferred_element_type=F32).astype(BF16)
@@ -318,21 +312,19 @@
                     src_ref=C.at[j], dst_ref=fin.at[2 * p + a], send_sem=f_send.at[j],
                     recv_sem=f_recv.at[2 * p + a], device_id=(row, cd, pd), device_id_type=MESH).start()
 
+    ring_step(1, 0)
+    ring_step(1, 1)
+    ring_step(2, 0)
+    ring_step(2, 1)
+    ring_step(3, 0)
+    ring_step(3, 1)
+    ring_step(4, 0)
+    cube_row(0)
+    ring_step(4, 1)
+    cube_row(1)
+
     def out_copy(i):
         return pltpu.make_async_copy(ob.at[i], out.at[i, 0], o_sem.at[i])
-
-    final_copy.wait()
-    for i in range(6):
-        @pl.when(jnp.logical_not((source_of(i) == c) & (i // 2 == p)))
-        def _():
-            pltpu.make_async_remote_copy(
-                src_ref=C.at[0], dst_ref=fin.at[i], send_sem=f_send.at[0], recv_sem=f_recv.at[i],
-                device_id=right, device_id_type=MESH).wait_recv()
-
-        keep = qm[0, i].astype(F32)
-        masked = xf[i] * xm[i, w_me].astype(F32)
-        ob[i] = keep * (1.5 * masked - (0.5 * norm) * fin[i].astype(F32))
-        out_copy(i).start()
 
     for h in range(6):
         on(h, halo_rep(h), s, lambda k, n: x_copy(h, s, k, n).wait_send())
@@ -352,6 +344,19 @@
             for way in range(2):
                 for a in halves(way, h):
                     ring_copy(way, h, a, o, source(way, h)).wait_send()
+    final_copy.wait()
+    for i in range(6):
+        @pl.when(jnp.logical_not((source_of(i) == c) & (i // 2 == p)))
+        def _():
+            pltpu.make_async_remote_copy(
+                src_ref=C.at[0], dst_ref=fin.at[i], send_sem=f_send.at[0], recv_sem=f_recv.at[i],
+                device_id=right, device_id_type=MESH).wait_recv()
+
+        keep = qm[0, i].astype(F32)
+        masked = xf[i] * xm[i, w_me].astype(F32)
+        ob[i] = keep * (1.5 * masked - (0.5 * norm) * fin[i].astype(F32))
+        out_copy(i).start()
+
     for j in range(6):
         @pl.when(jnp.logical_not(targets[j][3]))
         def _():

time: 65 us -> 63.8 us (0.982)
  Pallas kernels: 63 us -> 61.8 us
    pallas_call x1, Pallas kernels: 63 us -> 61.8 us  [body(): pl.pallas_call(run, out_shape=jax.ShapeDtypeStruct((rows, 1, T, T), F32),...]
where the time goes in v6:
time: 63.8 us; the launch traced here: 63.6 us
  Pallas kernels  61.8 us (97%)
  local copies, waits for them, and re-layouts  1.77 us (3%)
    pallas_call x1, Pallas kernels, body(): pl.pallas_call(run, out_shape=jax.ShapeDtypeStruct((rows, 1, T, T), F32),...  61.8 us
    unnamed x1, local copies, waits for them, and re-layouts  1.77 us

profile of v6, /device:TPU:8, one launch (start us, length us, event | category | flops | bytes accessed | tf_op | source)
XLA Modules:
  0.0 63.6 jit_solution(6039394496509068934)
XLA Ops:
  0.0 61.8 %sign_step.1 = f32[6,1,128,128]{3,2,1,0:T(8,128)} custom-call(s32[6,24]{1,0:T(8,128)} %refs_0_.1, s32[3,6]{1,0:T(4,128)} %bitcast.2, s32[1,6]{1,0:T(1,128)} %bitcast.3, f32[6,24,128,128]{3,2,1,0:T(8,128)} %refs_3_.1), custom_call_target="tpu_custom_call" | custom-call | tf_op jit(solution)/shard_map/sign_step/pallas_call | solution.py:378
  61.8 1.8 %copy.6 = f32[6,1,128,128]{3,2,1,0:T(8,128)} copy(f32[6,1,128,128]{3,2,1,0:T(8,128)} %sign_step.1) | data formatting | bytes 786432

commit v7 on v6

--- a/solution.py
+++ b/solution.py
@@ -187,7 +187,6 @@
     sib_copy(1, s).start()
     for h in (0, 5):
         make_halo(h)
-        x_start(h)
     rows_copy.wait()
 
     @pl.loop(0, BW)
@@ -195,6 +194,10 @@
         for a in range(2):
             L[a, :, pl.ds(pl.multiple_of(u * T, T), T)] = (xl[a, u] * scale_of(2 * p + a, u)).astype(BF16)
 
+    for h in (1, 3):
+        on(h, halo_rep(h), s, lambda k, n: x_copy(h, s, k, n).wait_send())
+    for h in (0, 5):
+        x_start(h)
     for m in (2, 0, 3):
         make_own(m)
         sib_copy(m, s).start()
@@ -326,7 +329,7 @@
     def out_copy(i):
         return pltpu.make_async_copy(ob.at[i], out.at[i, 0], o_sem.at[i])
 
-    for h in range(6):
+    for h in (0, 2, 4, 5):
         on(h, halo_rep(h), s, lambda k, n: x_copy(h, s, k, n).wait_send())
     for h in range(1, 5):
         on(h, p, s, lambda k, n: pass_copy(h, s, k, n).wait_send())

time: 63.8 us -> 63.8 us (level)
  no operation moved by 1% of the time
where the time goes in v7:
time: 63.8 us; the launch traced here: 63.5 us
  Pallas kernels  61.7 us (97%)
  local copies, waits for them, and re-layouts  1.77 us (3%)
    pallas_call x1, Pallas kernels, body(): pl.pallas_call(run, out_shape=jax.ShapeDtypeStruct((rows, 1, T, T), F32),...  61.7 us
    unnamed x1, local copies, waits for them, and re-layouts  1.77 us

profile of v7, /device:TPU:8, one launch (start us, length us, event | category | flops | bytes accessed | tf_op | source)
XLA Modules:
  0.0 63.5 jit_solution(14751574823760057678)
XLA Ops:
  0.0 61.7 %sign_step.1 = f32[6,1,128,128]{3,2,1,0:T(8,128)} custom-call(s32[6,24]{1,0:T(8,128)} %refs_0_.1, s32[3,6]{1,0:T(4,128)} %bitcast.2, s32[1,6]{1,0:T(1,128)} %bitcast.3, f32[6,24,128,128]{3,2,1,0:T(8,128)} %refs_3_.1), custom_call_target="tpu_custom_call" | custom-call | tf_op jit(solution)/shard_map/sign_step/pallas_call | solution.py:381
  61.8 1.8 %copy.6 = f32[6,1,128,128]{3,2,1,0:T(8,128)} copy(f32[6,1,128,128]{3,2,1,0:T(8,128)} %sign_step.1) | data formatting | bytes 786432
